TPU v7x, 32 devices: a whole 2x2x4 slice. The times are simulated.
32 devices in a mesh: group: 2 (over x), pos: 16 (over z, y, core).
Axes of the slice: x: 2, y: 2, z: 4, core: 2. Of those that a mesh axis runs over, the one named last changes fastest.
Arguments:
- acts: bfloat16 [4, 1024, 1536], P('group', 'pos'), parts along dimension 0, may hold values from -12 to 12
- skips: bfloat16 [4, 2048, 1280], P('group', 'pos'), parts along dimension 0, may hold values from -6 to 6
- norm_gain: float32 [1536], replicated, may hold values from 0.6 to 1.6
- w_query: bfloat16 [1536, 256], replicated, may hold values from -4 to 4
- w_key: bfloat16 [1536, 256], replicated, may hold values from -4 to 4
- w_value: bfloat16 [1536, 768], replicated, may hold values from -0.15625 to 0.15625
- w_out: bfloat16 [768, 1536], replicated, may hold values from -0.21875 to 0.21875
- w_lift: bfloat16 [1536, 1536], P('pos'), may hold values from -0.15625 to 0.15625
- w_skip: bfloat16 [1280, 1536], P('pos'), may hold values from -0.15625 to 0.15625
- depth_kernel: float32 [3, 1536], replicated, may hold values from -3 to 3
- w_point: bfloat16 [1536, 1536], P(None, 'pos'), may hold values from -0.15625 to 0.15625
Outputs:
- decoded: bfloat16 [4, 2048, 1536], P('group', 'pos'), parts along dimension 0
There are 2 independent parts, one for each index of `group`. A program takes and returns all parts, laid end to end along the dimension named above; an argument that names none is the same for every part. Nothing has to cross between parts.
All inputs are finite; a program needn't handle non-finite values.
Results may differ from a plain program's by a relative error of at most 0.014.
Values may be sent and summed in bfloat16 or wider, within the bound.
A program may use at most 128 MiB of HBM per device.

v0:
```python
import jax
import jax.numpy as jnp
from jax import lax
from jax.sharding import PartitionSpec as P

HEADS = 4
HK = 64
HV = 192


def extended(cells, sides, width):
    for axis, dim in sides:
        count = lax.axis_size(axis)
        ends = count - 1
        head = lax.slice_in_dim(cells, 0, width, axis=dim)
        tail = lax.slice_in_dim(cells, cells.shape[dim] - width, cells.shape[dim], axis=dim)
        cells = jnp.concatenate(
            [
                lax.ppermute(tail, axis, [(i, (i + 1) % count) for i in range(ends)]),
                cells,
                lax.ppermute(head, axis, [((i + 1) % count, i) for i in range(ends)]),
            ],
            axis=dim,
        )
    return cells


def on_device(
    acts, skips, norm_gain, w_query, w_key, w_value, w_out, w_lift, w_skip, depth_kernel, w_point
):
    lift_full, skip_full, point_full = (
        lax.all_gather(w_lift, "pos", axis=0, tiled=True),
        lax.all_gather(w_skip, "pos", axis=0, tiled=True),
        lax.all_gather(w_point, "pos", axis=1, tiled=True),
    )
    seq_count, bin_rows, width = acts.shape
    actsf = acts.astype(jnp.float32)
    centre = actsf - jnp.mean(actsf, axis=-1, keepdims=True)
    normed = (
        centre * lax.rsqrt(jnp.mean(centre * centre, axis=-1, keepdims=True) + 1e-05) * norm_gain
    ).astype(jnp.bfloat16)
    flat = normed.reshape(seq_count * bin_rows, width)
    queries = (
        (jnp.dot(flat, w_query, preferred_element_type=jnp.float32) * HK ** (-0.5))
        .astype(jnp.bfloat16)
        .reshape(seq_count, bin_rows, HEADS, HK)
    )
    keys_here = (
        jnp.dot(flat, w_key, preferred_element_type=jnp.float32)
        .astype(jnp.bfloat16)
        .reshape(seq_count, bin_rows, HEADS * HK)
    )
    values_here = (
        jnp.dot(flat, w_value, preferred_element_type=jnp.float32)
        .astype(jnp.bfloat16)
        .reshape(seq_count, bin_rows, HEADS * HV)
    )
    running = jnp.full((seq_count, HEADS, bin_rows), -1e30, jnp.float32)
    key_piece = lax.all_gather(keys_here, "pos", axis=1, tiled=True)
    value_piece = lax.all_gather(values_here, "pos", axis=1, tiled=True)
    count = key_piece.shape[1]
    keyed = key_piece.reshape(seq_count, count, HEADS, HK)
    valued = value_piece.reshape(seq_count, count, HEADS, HV)
    scores = jnp.einsum("sqhd,skhd->shqk", queries, keyed, preferred_element_type=jnp.float32)
    newest = jnp.maximum(running, jnp.max(scores, axis=-1))
    weights = jnp.exp(scores - newest[..., None])
    totals = jnp.sum(weights, axis=-1)
    summed = jnp.einsum(
        "shqk,skhv->shqv", weights.astype(jnp.bfloat16), valued, preferred_element_type=jnp.float32
    )
    running, totals, summed = (newest, totals, summed)
    mixed = (
        (summed / totals[..., None])
        .transpose(0, 2, 1, 3)
        .reshape(seq_count * bin_rows, HEADS * HV)
        .astype(jnp.bfloat16)
    )
    attended = (
        actsf.reshape(seq_count * bin_rows, width)
        + jnp.dot(mixed, w_out, preferred_element_type=jnp.float32)
    ).astype(jnp.bfloat16)
    activated = jax.nn.gelu(attended.astype(jnp.float32)).astype(jnp.bfloat16)
    lifted = jnp.dot(activated, lift_full, preferred_element_type=jnp.float32)
    lifted = lifted.astype(jnp.bfloat16).reshape(seq_count, bin_rows, width)
    raised = jnp.repeat(lifted, 2, axis=1).reshape(seq_count * 2 * bin_rows, width)
    skip_act = (
        jax.nn.gelu(skips.astype(jnp.float32))
        .astype(jnp.bfloat16)
        .reshape(seq_count * 2 * bin_rows, skips.shape[2])
    )
    skip_term = jnp.dot(skip_act, skip_full, preferred_element_type=jnp.float32)
    merged = (
        (raised.astype(jnp.float32) + skip_term)
        .astype(jnp.bfloat16)
        .reshape(seq_count, 2 * bin_rows, width)
    )
    padded = extended(merged, (("pos", 1),), 1)
    paddedf = padded.astype(jnp.float32)
    spread = (
        depth_kernel[0] * paddedf[:, :-2]
        + depth_kernel[1] * paddedf[:, 1:-1]
        + depth_kernel[2] * paddedf[:, 2:]
    ).astype(jnp.bfloat16)
    spread = spread.reshape(seq_count * 2 * bin_rows, width)
    decoded = jnp.dot(spread, point_full, preferred_element_type=jnp.float32)
    return decoded.astype(jnp.bfloat16).reshape(seq_count, 2 * bin_rows, width)


def solution(mesh):
    return jax.shard_map(
        on_device,
        mesh=mesh,
        in_specs=(
            P("group", "pos", None),
            P("group", "pos", None),
            P(),
            P(),
            P(),
            P(),
            P(),
            P("pos", None),
            P("pos", None),
            P(),
            P(None, "pos"),
        ),
        out_specs=P("group", "pos", None),
        check_vma=False,
    )
```

profile of v0, /device:TPU:0, one launch (start us, length us, event | category | flops | bytes accessed | tf_op | source)
XLA Modules:
  0.0 268.4 jit_solution(8063212985456525454)
XLA Ops:
  6.5 0.0 copy-start
  6.5 0.0 all-gather.6.cloned.1.call-start
  6.5 1.3 convert_reduce_fusion
  7.8 1.3 multiply_reduce_fusion
  9.1 1.3 multiply_convert_fusion
  10.4 0.0 copy-done.3
  10.4 0.9 convolution_convert_fusion.3
  11.3 0.0 all-gather.6.cloned.1.call-update
  11.3 0.0 copy-start.4
  11.3 0.0 all-gather.8.cloned.1.call-start
  11.4 2.9 %convolution_convert_fusion.2 = bf16[128,768]{1,0:T(8,128)(2,1)} fusion(bf16[128,1536]{1,0:T(8,128)(2,1)S(1)} %bitcast.36, bf16[1536,768]{1,0:T(8,128)(2,1)} %param.16), kind=kOutput, calls=%fused_computation.30 | convolution fusion | flops 302088192 | bytes 2949120 | tf_op jit(solution)/shard_map/dot_general | solution.py:54
  14.3 0.0 all-gather.8.cloned.1.call-update
  14.3 0.0 all-gather.10.cloned.1.call-start
  14.3 0.7 all-gather.10.cloned.1.call-update
  15.0 0.0 all-gather.12.cloned.1.call-start
  15.1 0.5 all-gather.12.cloned.1.call-update
  15.6 0.0 all-gather.14.cloned.1.call-start
  15.6 0.5 all-gather.14.cloned.1.call-update
  16.2 0.9 fusion.16
  17.1 1.0 reshape.61
  18.1 2.4 fusion.13
  20.4 31.7 %all-gather.6.cloned.1.call-done = bf16[2,1024,256]{2,1,0:T(8,128)(2,1)} async-done(((bf16[2,64,256]{2,1,0:T(8,128)(2,1)}), bf16[2,1024,256]{2,1,0:T(8,128)(2,1)}) %all-gather.6.cloned.1.call-update) | async-done | bytes 1048592 | tf_op jit(solution)/shard_map/all_gather | solution.py:59
  52.1 1.5 copy.15
  53.6 0.5 fusion.38
  54.1 0.0 copy-start.1
  54.1 1.3 copy-done.1
  55.5 0.5 fusion.3
  56.0 42.6 %all-gather.8.cloned.1.call-done = bf16[2,1024,768]{2,1,0:T(8,128)(2,1)} async-done(((bf16[2,64,768]{2,1,0:T(8,128)(2,1)}), bf16[2,1024,768]{2,1,0:T(8,128)(2,1)}) %all-gather.8.cloned.1.call-update) | async-done | bytes 3145744 | tf_op jit(solution)/shard_map/all_gather | solution.py:60
  98.6 4.6 %copy.17 = bf16[2,1024,768]{1,2,0:T(8,128)(2,1)} copy(bf16[2,1024,768]{2,1,0:T(8,128)(2,1)} %all-gather.8.cloned.1.call-done) | data formatting | bytes 6291456 | tf_op jit(solution)/shard_map/all_gather | solution.py:60
  103.2 3.7 %fusion.15 = bf16[2,64,4,192]{3,1,2,0:T(8,128)(2,1)S(1)} fusion(bf16[2,1024,4,192]{1,3,2,0:T(8,128)(2,1)} %bitcast.40, f32[2,4,64,1024]{3,2,1,0:T(8,128)} %copy-done.1, f32[2,4,64]{2,1,0:T(4,128)S(1)} %broadcast_maximum_fusion, f32[2,64,4]{1,2,0:T(4,128)S(1)} %bitcast.48), kind=kOutput, calls=%fused_computation.28 | convolution fusion | flops 202571776 | bytes 5443584 | tf_op jit(solution)/shard_map/shqk,skhv->shqv/dot_general | solution.py:68
  106.9 0.2 copy.18
  107.2 0.2 convert_element_type.71
  107.4 45.7 %all-gather.10.cloned.1.call-done = bf16[1536,1536]{1,0:T(8,128)(2,1)} async-done(((bf16[96,1536]{1,0:T(8,128)(2,1)}), bf16[1536,1536]{1,0:T(8,128)(2,1)}) %all-gather.10.cloned.1.call-update) | async-done | bytes 4718608 | tf_op jit(solution)/shard_map/all_gather | solution.py:32
  153.1 3.7 %convolution_convert_fusion.1 = bf16[128,1536]{1,0:T(8,128)(2,1)S(1)} fusion(bf16[1536,1536]{1,0:T(8,128)(2,1)} %all-gather.10.cloned.1.call-done, bf16[128,768]{1,0:T(8,128)(2,1)S(1)} %convert_element_type.71, bf16[768,1536]{1,0:T(8,128)(2,1)S(1)} %copy-done, bf16[128,1536]{1,0:T(8,128)(2,1)S(1)} %bitcast.39), kind=kOutput, calls=%fused_computation.6 | convolution fusion | flops 908722176 | bytes 8060928 | tf_op jit(solution)/shard_map/dot_general | solution.py:83
  156.8 1.6 broadcast_in_dim.5
  158.3 3.2 %convert_element_type.78 = f32[256,1536]{1,0:T(8,128)} reshape(f32[2,64,2,1536]{3,2,1,0:T(2,128)} %broadcast_in_dim.5) | data formatting | bytes 3145728 | tf_op jit(solution)/shard_map/convert_element_type | solution.py:93
  161.5 41.0 %all-gather.12.cloned.1.call-done = bf16[1280,1536]{1,0:T(8,128)(2,1)} async-done(((bf16[80,1536]{1,0:T(8,128)(2,1)}), bf16[1280,1536]{1,0:T(8,128)(2,1)}) %all-gather.12.cloned.1.call-update) | async-done | bytes 3932176 | tf_op jit(solution)/shard_map/all_gather | solution.py:33
  202.6 3.8 %fusion = bf16[256,1536]{1,0:T(8,128)(2,1)S(1)} fusion(f32[256,1536]{1,0:T(8,128)} %convert_element_type.78, bf16[256,1280]{1,0:T(8,128)(2,1)S(1)} %bitcast.45, bf16[1280,1536]{1,0:T(8,128)(2,1)} %all-gather.12.cloned.1.call-done), kind=kOutput, calls=%fused_computation.1 | convolution fusion | flops 1007419392 | bytes 6946816 | tf_op jit(solution)/shard_map/dot_general | solution.py:91
  206.4 2.2 collective-permute-start
  208.6 1.3 collective-permute-start.1
  209.9 0.0 copy-done.6
  209.9 0.1 slice_reduce_fusion.2
  209.9 0.0 collective-permute-done
  210.0 1.7 collective-permute-done.1
  211.7 0.2 maximum_convert_fusion
  211.9 0.5 fusion.6
  212.4 44.8 %all-gather.14.cloned.1.call-done = bf16[1536,1536]{0,1:T(8,128)(2,1)} async-done(((bf16[1536,96]{0,1:T(8,128)(2,1)}), bf16[1536,1536]{0,1:T(8,128)(2,1)}) %all-gather.14.cloned.1.call-update) | async-done | bytes 4718608 | tf_op jit(solution)/shard_map/all_gather | solution.py:34
  257.2 4.6 %convolution_convert_fusion = bf16[256,1536]{1,0:T(8,128)(2,1)} fusion(bf16[256,1536]{1,0:T(8,128)(2,1)S(1)} %bitcast.44, bf16[1536,1536]{0,1:T(8,128)(2,1)} %all-gather.14.cloned.1.call-done), kind=kOutput, calls=%fused_computation.2 | convolution fusion | flops 1208352768 | bytes 6291456 | tf_op jit(solution)/shard_map/dot_general | solution.py:105
  (12 shorter events, 0.1 us)
Async XLA Ops:
  6.5 146.6 %copy-start = (bf16[768,1536]{1,0:T(8,128)(2,1)S(1)}, bf16[768,1536]{1,0:T(8,128)(2,1)}, u32[]{:S(2)}) copy-start(bf16[768,1536]{1,0:T(8,128)(2,1)} %param.17) | copy-start | bytes 7077892
  6.5 3.8 %copy-start.3 = (bf16[1536,256]{1,0:T(8,128)(2,1)S(1)}, bf16[1536,256]{1,0:T(8,128)(2,1)}, u32[]{:S(2)}) copy-start(bf16[1536,256]{1,0:T(8,128)(2,1)} %param.15) | copy-start | bytes 2359300
  6.5 45.6 %all-gather.6.cloned.1.call-start = ((), (), s32[]{:S(2)}) async-start(), calls=%async_computation | async-start | bytes 1114112 | tf_op jit(solution)/shard_map/all_gather | solution.py:59
  11.3 4.9 %copy-start.4 = (bf16[1536,256]{1,0:T(8,128)(2,1)S(1)}, bf16[1536,256]{1,0:T(8,128)(2,1)}, u32[]{:S(2)}) copy-start(bf16[1536,256]{1,0:T(8,128)(2,1)} %param.14) | copy-start | bytes 2359300
  11.3 87.3 %all-gather.8.cloned.1.call-start = ((), (), s32[]{:S(2)}) async-start(), calls=%async_computation.1 | async-start | bytes 3342336 | tf_op jit(solution)/shard_map/all_gather | solution.py:60
  14.3 138.8 %all-gather.10.cloned.1.call-start = ((), (), s32[]{:S(2)}) async-start(), calls=%async_computation.2 | async-start | bytes 5013504 | tf_op jit(solution)/shard_map/all_gather | solution.py:32
  15.0 187.6 %all-gather.12.cloned.1.call-start = ((), (), s32[]{:S(2)}) async-start(), calls=%async_computation.3 | async-start | bytes 4177920 | tf_op jit(solution)/shard_map/all_gather | solution.py:33
  15.6 241.7 %all-gather.14.cloned.1.call-start = ((), (), s32[]{:S(2)}) async-start(), calls=%async_computation.4 | async-start | bytes 5013504 | tf_op jit(solution)/shard_map/all_gather | solution.py:34
  54.1 1.4 copy-start.1
  103.2 49.9 %copy-start.2 = (bf16[2,64,1536]{2,1,0:T(8,128)(2,1)S(1)}, bf16[2,64,1536]{2,1,0:T(8,128)(2,1)}, u32[]{:S(2)}) copy-start(bf16[2,64,1536]{2,1,0:T(8,128)(2,1)} %param.11) | copy-start | bytes 1179652
  158.3 44.3 %copy-start.5 = (bf16[2,128,1280]{2,1,0:T(8,128)(2,1)S(1)}, bf16[2,128,1280]{2,1,0:T(8,128)(2,1)}, u32[]{:S(2)}) copy-start(bf16[2,128,1280]{2,1,0:T(8,128)(2,1)} %fusion.13) | copy-start | bytes 1966084
  202.6 7.3 %copy-start.6 = (f32[3,1536]{1,0:T(4,128)S(1)}, f32[3,1536]{1,0:T(4,128)}, u32[]{:S(2)}) copy-start(f32[3,1536]{1,0:T(4,128)} %param.20) | copy-start | bytes 55300
  206.4 3.5 %collective-permute-start = (bf16[2,1,1536]{2,1,0:T(2,128)(2,1)S(1)}, bf16[2,1,1536]{2,1,0:T(2,128)(2,1)S(1)}, u32[]{:S(2)}, u32[]{:S(2)}) collective-permute-start(bf16[2,1,1536]{2,1,0:T(2,128)(2,1)S(1)} %get-tuple-element.8), channel_id=1, source_target_pairs={{0,1},{1,2},{2,3},{3,4},{4,5},{5,6},{6,7},{7,8},{8,9},{9,10},{10,1... | collective-permute-start | bytes 18440 | tf_op jit(solution)/shard_map/ppermute | solution.py:19
  208.6 3.1 %collective-permute-start.1 = (bf16[2,1,1536]{2,1,0:T(2,128)(2,1)S(1)}, bf16[2,1,1536]{2,1,0:T(2,128)(2,1)S(1)}, u32[]{:S(2)}, u32[]{:S(2)}) collective-permute-start(bf16[2,1,1536]{2,1,0:T(2,128)(2,1)S(1)} %get-tuple-element.9), channel_id=1, source_target_pairs={{1,0},{2,1},{3,2},{4,3},{5,4},{6,5},{7,6},{8,7},{9,8},{10,9},{11,1... | collective-permute-start | bytes 18440 | tf_op jit(solution)/shard_map/ppermute | solution.py:21
Sparse Core Ops, SparseCore 0:
  11.4 40.6 all-gather.5
  54.4 44.1 all-gather.7
  100.9 52.1 all-gather.9
  155.2 47.3 all-gather.11
  204.7 52.4 all-gather.13
where the time goes:
time: 269 us; the launch traced here: 268 us
  waiting for transfers between devices  209 us (78%)
  matrix products  21 us (8%)
  local copies, waits for them, and re-layouts  13.7 us (5%)
  between operations  13.3 us (5%)
  other arithmetic  7.44 us (3%)
  starting transfers between devices  3.61 us (1%)
    all_gather x1, waiting for transfers between devices, on_device(): lax.all_gather(w_lift, 'pos', axis=0, tiled=True)  45.7 us
    all_gather x1, waiting for transfers between devices, on_device(): lax.all_gather(w_point, 'pos', axis=1, tiled=True)  44.8 us
    all_gather x1, waiting for transfers between devices, on_device(): value_piece = lax.all_gather(values_here, 'pos', axis=1, tiled=True)  42.6 us
    all_gather x1, waiting for transfers between devices, on_device(): lax.all_gather(w_skip, 'pos', axis=0, tiled=True)  41 us
    all_gather x1, waiting for transfers between devices, on_device(): key_piece = lax.all_gather(keys_here, 'pos', axis=1, tiled=True)  31.7 us
  transfers between devices with their start and end apart: 7, of which 6 were waited for; matrix products, arithmetic and copies ran while one was open for 12% of the time, Pallas kernels for 0%

commit v1 on v0

--- a/solution.py
+++ b/solution.py
@@ -56,7 +56,14 @@
         .reshape(seq_count, bin_rows, HEADS * HV)
     )
     running = jnp.full((seq_count, HEADS, bin_rows), -1e30, jnp.float32)
-    key_piece = lax.all_gather(keys_here, "pos", axis=1, tiled=True)
+    ways, here = (lax.axis_size("pos"), lax.axis_index("pos"))
+    key_piece, reach = (keys_here, 1)
+    while reach < ways:
+        theirs = lax.ppermute(key_piece, "pos", [(d, d ^ reach) for d in range(ways)])
+        mine_first = jnp.concatenate([key_piece, theirs], axis=1)
+        theirs_first = jnp.concatenate([theirs, key_piece], axis=1)
+        key_piece = jnp.where(here & reach == 0, mine_first, theirs_first)
+        reach = 2 * reach
     value_piece = lax.all_gather(values_here, "pos", axis=1, tiled=True)
     count = key_piece.shape[1]
     keyed = key_piece.reshape(seq_count, count, HEADS, HK)

time: 269 us -> 248 us (0.922)
  waiting for transfers between devices: 209 us -> 174 us
  starting transfers between devices: 3.61 us -> 11.5 us
  other arithmetic: 7.44 us -> 10.7 us
    ppermute x0 -> x4, waiting for transfers between devices: none -> 44.3 us  [on_device(): lax.ppermute(key_piece, 'pos', [(d, d ^ reach) for d in range(ways)])]
    all_gather x1, waiting for transfers between devices: 42.6 us -> 0.02 us  [on_device(): value_piece = lax.all_gather(values_here, 'pos', axis=1, tiled=True)]
    all_gather x1 -> x0, waiting for transfers between devices: 31.7 us -> none  [on_device(): key_piece = lax.all_gather(keys_here, 'pos', axis=1, tiled=True)]
    ppermute x0 -> x4, starting transfers between devices: none -> 7.91 us  [on_device(): lax.ppermute(key_piece, 'pos', [(d, d ^ reach) for d in range(ways)])]
    all_gather x1, waiting for transfers between devices: 45.7 us -> 40.1 us  [on_device(): lax.all_gather(w_lift, 'pos', axis=0, tiled=True)]
    select_n x0 -> x6, other arithmetic: none -> 3.23 us  [on_device(): key_piece = jnp.where(here & reach == 0, mine_first, theirs_first)]
  transfers between devices with their start and end apart: 7 -> 10, of which waited for: 6 -> 8; matrix products, arithmetic and copies ran while one was open for 12% -> 14% of each run, Pallas kernels for 0% -> 0%
where the time goes in v1:
time: 248 us; the launch traced here: 247 us
  waiting for transfers between devices  174 us (70%)
  matrix products  22.9 us (9%)
  local copies, waits for them, and re-layouts  14.8 us (6%)
  between operations  13.4 us (5%)
  starting transfers between devices  11.5 us (5%)
  other arithmetic  10.7 us (4%)
    all_gather x1, waiting for transfers between devices, on_device(): lax.all_gather(w_point, 'pos', axis=1, tiled=True)  44.9 us
    ppermute x4, waiting for transfers between devices, on_device(): lax.ppermute(key_piece, 'pos', [(d, d ^ reach) for d in range(ways)])  44.3 us
    all_gather x1, waiting for transfers between devices, on_device(): lax.all_gather(w_skip, 'pos', axis=0, tiled=True)  41.1 us
    all_gather x1, waiting for transfers between devices, on_device(): lax.all_gather(w_lift, 'pos', axis=0, tiled=True)  40.1 us
    ppermute x4, starting transfers between devices, on_device(): lax.ppermute(key_piece, 'pos', [(d, d ^ reach) for d in range(ways)])  7.91 us
  transfers between devices with their start and end apart: 10, of which 8 were waited for; matrix products, arithmetic and copies ran while one was open for 14% of the time, Pallas kernels for 0%

profile of v1, /device:TPU:0, one launch (start us, length us, event | category | flops | bytes accessed | tf_op | source)
XLA Modules:
  0.0 247.2 jit_solution(17950774414102457658)
XLA Ops:
  6.5 1.3 convert_reduce_fusion
  7.8 1.3 multiply_reduce_fusion
  9.1 1.3 multiply_convert_fusion
  10.4 2.9 %convolution_convert_fusion.2 = bf16[128,768]{1,0:T(8,128)(2,1)} fusion(bf16[128,1536]{1,0:T(8,128)(2,1)S(1)} %bitcast.37, bf16[1536,768]{1,0:T(8,128)(2,1)} %param.16), kind=kOutput, calls=%fused_computation.30 | convolution fusion | flops 302088192 | bytes 2949120 | tf_op jit(solution)/shard_map/dot_general | solution.py:54
  13.4 0.7 all-gather.7.cloned.1.call-update
  14.1 0.7 all-gather.9.cloned.1.call-update
  14.8 0.5 all-gather.11.cloned.1.call-update
  15.4 0.9 convolution_convert_fusion.3
  16.3 0.5 collective-permute-start
  16.7 1.1 collective-permute-done
  17.9 1.0 maximum_select_fusion.7
  18.8 2.9 %collective-permute-start.1 = (bf16[2,128,256]{2,1,0:T(8,128)(2,1)S(1)}, bf16[2,128,256]{2,1,0:T(8,128)(2,1)S(1)}, u32[]{:S(2)}, u32[]{:S(2)}) collective-permute-start(bf16[2,128,256]{2,1,0:T(8,128)(2,1)S(1)} %maximum_select_fusion.7), channel_id=1, source_target_pairs={{0,2},{1,3},{2,0},{3,1},{4,6},{5,7},{6,4},{7,5},{8,10},{9,11},{10,... | collective-permute-start | bytes 393224 | tf_op jit(solution)/shard_map/ppermute | solution.py:62
  21.7 1.0 concatenate.57
  22.7 0.1 copy.21
  22.9 2.7 %collective-permute-done.1 = bf16[2,128,256]{2,1,0:T(8,128)(2,1)S(1)} collective-permute-done((bf16[2,128,256]{2,1,0:T(8,128)(2,1)S(1)}, bf16[2,128,256]{2,1,0:T(8,128)(2,1)S(1)}, u32[]{:S(2)}, u32[]{:S(2)}) %collective-permute-start.1) | collective-permute-done | bytes 131104 | tf_op jit(solution)/shard_map/ppermute | solution.py:62
  25.7 1.9 collective-permute-start.2
  27.5 2.4 fusion.13
  29.9 8.7 %collective-permute-done.2 = bf16[2,256,256]{2,1,0:T(8,128)(2,1)S(1)} collective-permute-done((bf16[2,256,256]{2,1,0:T(8,128)(2,1)S(1)}, bf16[2,256,256]{2,1,0:T(8,128)(2,1)S(1)}, u32[]{:S(2)}, u32[]{:S(2)}) %collective-permute-start.2) | collective-permute-done | bytes 262176 | tf_op jit(solution)/shard_map/ppermute | solution.py:62
  38.6 1.0 maximum_select_fusion.3
  39.6 2.7 %collective-permute-start.3 = (bf16[2,512,256]{2,1,0:T(8,128)(2,1)}, bf16[2,512,256]{2,1,0:T(8,128)(2,1)}, u32[]{:S(2)}, u32[]{:S(2)}) collective-permute-start(bf16[2,512,256]{2,1,0:T(8,128)(2,1)} %maximum_select_fusion.3), channel_id=1, source_target_pairs={{0,8},{1,9},{2,10},{3,11},{4,12},{5,13},{6,14},{7,15},{8,0},{9,1},... | collective-permute-start | bytes 1572872 | tf_op jit(solution)/shard_map/ppermute | solution.py:62
  42.2 1.4 fusion.16
  43.8 0.1 copy.20
  43.9 0.2 maximum_select_fusion.6
  44.1 0.1 copy.23
  44.3 0.1 copy.24
  44.4 0.9 maximum_select_fusion.2
  45.4 31.8 %collective-permute-done.3 = bf16[2,512,256]{2,1,0:T(8,128)(2,1)} collective-permute-done((bf16[2,512,256]{2,1,0:T(8,128)(2,1)}, bf16[2,512,256]{2,1,0:T(8,128)(2,1)}, u32[]{:S(2)}, u32[]{:S(2)}) %collective-permute-start.3) | collective-permute-done | bytes 524320 | tf_op jit(solution)/shard_map/ppermute | solution.py:62
  77.2 1.3 copy.25
  78.4 1.7 fusion.45
  80.2 1.3 copy-done.2
  81.6 0.5 fusion.3
  82.1 4.7 %copy.27 = bf16[2,1024,768]{1,2,0:T(8,128)(2,1)} copy(bf16[2,1024,768]{2,1,0:T(8,128)(2,1)} %all-gather.5.cloned.1.call-done) | data formatting | bytes 6291456 | tf_op jit(solution)/shard_map/all_gather | solution.py:67
  86.8 3.7 %fusion.15 = bf16[2,64,4,192]{3,1,2,0:T(8,128)(2,1)S(1)} fusion(bf16[2,1024,4,192]{1,3,2,0:T(8,128)(2,1)} %bitcast.41, f32[2,4,64,1024]{3,2,1,0:T(8,128)} %copy-done.2, f32[2,4,64]{2,1,0:T(4,128)S(1)} %broadcast_maximum_fusion, f32[2,64,4]{1,2,0:T(4,128)S(1)} %bitcast.52), kind=kOutput, calls=%fused_computation.28 | convolution fusion | flops 202571776 | bytes 5443584 | tf_op jit(solution)/shard_map/shqk,skhv->shqv/dot_general | solution.py:75
  90.5 0.2 copy.28
  90.7 0.9 convert_element_type.71
  91.6 40.1 %all-gather.7.cloned.1.call-done = bf16[1536,1536]{1,0:T(8,128)(2,1)} async-done(((bf16[96,1536]{1,0:T(8,128)(2,1)}), bf16[1536,1536]{1,0:T(8,128)(2,1)}) %all-gather.7.cloned.1.call-update) | async-done | bytes 4718608 | tf_op jit(solution)/shard_map/all_gather | solution.py:32
  131.8 3.8 %convolution_convert_fusion.1 = bf16[128,1536]{1,0:T(8,128)(2,1)S(1)} fusion(bf16[1536,1536]{1,0:T(8,128)(2,1)} %all-gather.7.cloned.1.call-done, bf16[128,768]{1,0:T(8,128)(2,1)} %convert_element_type.71, bf16[768,1536]{1,0:T(8,128)(2,1)S(1)} %copy-done, bf16[128,1536]{1,0:T(8,128)(2,1)S(1)} %bitcast.40), kind=kOutput, calls=%fused_computation.6 | convolution fusion | flops 908722176 | bytes 8060928 | tf_op jit(solution)/shard_map/dot_general | solution.py:90
  135.6 1.6 broadcast_in_dim.5
  137.1 3.1 %convert_element_type.78 = f32[256,1536]{1,0:T(8,128)} reshape(f32[2,64,2,1536]{3,2,1,0:T(2,128)} %broadcast_in_dim.5) | data formatting | bytes 3145728 | tf_op jit(solution)/shard_map/convert_element_type | solution.py:100
  140.3 41.1 %all-gather.9.cloned.1.call-done = bf16[1280,1536]{1,0:T(8,128)(2,1)} async-done(((bf16[80,1536]{1,0:T(8,128)(2,1)}), bf16[1280,1536]{1,0:T(8,128)(2,1)}) %all-gather.9.cloned.1.call-update) | async-done | bytes 3932176 | tf_op jit(solution)/shard_map/all_gather | solution.py:33
  181.4 3.8 %fusion = bf16[256,1536]{1,0:T(8,128)(2,1)S(1)} fusion(f32[256,1536]{1,0:T(8,128)} %convert_element_type.78, bf16[256,1280]{1,0:T(8,128)(2,1)S(1)} %bitcast.47, bf16[1280,1536]{1,0:T(8,128)(2,1)} %all-gather.9.cloned.1.call-done), kind=kOutput, calls=%fused_computation.1 | convolution fusion | flops 1007419392 | bytes 6946816 | tf_op jit(solution)/shard_map/dot_general | solution.py:98
  185.2 2.2 collective-permute-start.4
  187.4 1.3 collective-permute-start.5
  188.8 1.7 collective-permute-done.5
  190.5 0.2 maximum_convert_fusion
  190.7 0.5 fusion.6
  191.2 44.9 %all-gather.11.cloned.1.call-done = bf16[1536,1536]{0,1:T(8,128)(2,1)} async-done(((bf16[1536,96]{0,1:T(8,128)(2,1)}), bf16[1536,1536]{0,1:T(8,128)(2,1)}) %all-gather.11.cloned.1.call-update) | async-done | bytes 4718608 | tf_op jit(solution)/shard_map/all_gather | solution.py:34
  236.1 4.6 %convolution_convert_fusion = bf16[256,1536]{1,0:T(8,128)(2,1)} fusion(bf16[256,1536]{1,0:T(8,128)(2,1)S(1)} %bitcast.46, bf16[1536,1536]{0,1:T(8,128)(2,1)} %all-gather.11.cloned.1.call-done), kind=kOutput, calls=%fused_computation.2 | convolution fusion | flops 1208352768 | bytes 6291456 | tf_op jit(solution)/shard_map/dot_general | solution.py:112
  (26 shorter events, 0.6 us)
Async XLA Ops:
  6.5 125.2 %copy-start = (bf16[768,1536]{1,0:T(8,128)(2,1)S(1)}, bf16[768,1536]{1,0:T(8,128)(2,1)}, u32[]{:S(2)}) copy-start(bf16[768,1536]{1,0:T(8,128)(2,1)} %param.17) | copy-start | bytes 7077892
  6.5 75.6 %all-gather.5.cloned.1.call-start = ((), (), s32[]{:S(2)}) async-start(), calls=%async_computation | async-start | bytes 3342336 | tf_op jit(solution)/shard_map/all_gather | solution.py:67
  10.4 5.0 %copy-start.3 = (bf16[1536,256]{1,0:T(8,128)(2,1)S(1)}, bf16[1536,256]{1,0:T(8,128)(2,1)}, u32[]{:S(2)}) copy-start(bf16[1536,256]{1,0:T(8,128)(2,1)} %param.15) | copy-start | bytes 2359300
  13.3 118.5 %all-gather.7.cloned.1.call-start = ((), (), s32[]{:S(2)}) async-start(), calls=%async_computation.1 | async-start | bytes 5013504 | tf_op jit(solution)/shard_map/all_gather | solution.py:32
  14.1 167.4 %all-gather.9.cloned.1.call-start = ((), (), s32[]{:S(2)}) async-start(), calls=%async_computation.2 | async-start | bytes 4177920 | tf_op jit(solution)/shard_map/all_gather | solution.py:33
  14.8 221.3 %all-gather.11.cloned.1.call-start = ((), (), s32[]{:S(2)}) async-start(), calls=%async_computation.3 | async-start | bytes 5013504 | tf_op jit(solution)/shard_map/all_gather | solution.py:34
  16.3 1.6 collective-permute-start
  18.8 6.8 %collective-permute-start.1 = (bf16[2,128,256]{2,1,0:T(8,128)(2,1)S(1)}, bf16[2,128,256]{2,1,0:T(8,128)(2,1)S(1)}, u32[]{:S(2)}, u32[]{:S(2)}) collective-permute-start(bf16[2,128,256]{2,1,0:T(8,128)(2,1)S(1)} %maximum_select_fusion.7), channel_id=1, source_target_pairs={{0,2},{1,3},{2,0},{3,1},{4,6},{5,7},{6,4},{7,5},{8,10},{9,11},{10,... | collective-permute-start | bytes 393224 | tf_op jit(solution)/shard_map/ppermute | solution.py:62
  25.7 12.9 %collective-permute-start.2 = (bf16[2,256,256]{2,1,0:T(8,128)(2,1)S(1)}, bf16[2,256,256]{2,1,0:T(8,128)(2,1)S(1)}, u32[]{:S(2)}, u32[]{:S(2)}) collective-permute-start(bf16[2,256,256]{2,1,0:T(8,128)(2,1)S(1)} %maximum_select_fusion.5), channel_id=1, source_target_pairs={{0,4},{1,5},{2,6},{3,7},{4,0},{5,1},{6,2},{7,3},{8,12},{9,13},{10,... | collective-permute-start | bytes 786440 | tf_op jit(solution)/shard_map/ppermute | solution.py:62
  39.6 37.6 %collective-permute-start.3 = (bf16[2,512,256]{2,1,0:T(8,128)(2,1)}, bf16[2,512,256]{2,1,0:T(8,128)(2,1)}, u32[]{:S(2)}, u32[]{:S(2)}) collective-permute-start(bf16[2,512,256]{2,1,0:T(8,128)(2,1)} %maximum_select_fusion.3), channel_id=1, source_target_pairs={{0,8},{1,9},{2,10},{3,11},{4,12},{5,13},{6,14},{7,15},{8,0},{9,1},... | collective-permute-start | bytes 1572872 | tf_op jit(solution)/shard_map/ppermute | solution.py:62
  80.2 1.4 copy-start.2
  86.8 45.0 %copy-start.1 = (bf16[2,64,1536]{2,1,0:T(8,128)(2,1)S(1)}, bf16[2,64,1536]{2,1,0:T(8,128)(2,1)}, u32[]{:S(2)}) copy-start(bf16[2,64,1536]{2,1,0:T(8,128)(2,1)} %param.11) | copy-start | bytes 1179652
  135.6 45.8 %copy-start.4 = (bf16[2,128,1280]{2,1,0:T(8,128)(2,1)S(1)}, bf16[2,128,1280]{2,1,0:T(8,128)(2,1)}, u32[]{:S(2)}) copy-start(bf16[2,128,1280]{2,1,0:T(8,128)(2,1)} %fusion.13) | copy-start | bytes 1966084
  181.4 7.3 %copy-start.5 = (f32[3,1536]{1,0:T(4,128)S(1)}, f32[3,1536]{1,0:T(4,128)}, u32[]{:S(2)}) copy-start(f32[3,1536]{1,0:T(4,128)} %param.20) | copy-start | bytes 55300
  185.2 3.5 %collective-permute-start.4 = (bf16[2,1,1536]{2,1,0:T(2,128)(2,1)S(1)}, bf16[2,1,1536]{2,1,0:T(2,128)(2,1)S(1)}, u32[]{:S(2)}, u32[]{:S(2)}) collective-permute-start(bf16[2,1,1536]{2,1,0:T(2,128)(2,1)S(1)} %get-tuple-element.8), channel_id=1, source_target_pairs={{0,1},{1,2},{2,3},{3,4},{4,5},{5,6},{6,7},{7,8},{8,9},{9,10},{10,1... | collective-permute-start | bytes 18440 | tf_op jit(solution)/shard_map/ppermute | solution.py:19
  187.4 3.1 %collective-permute-start.5 = (bf16[2,1,1536]{2,1,0:T(2,128)(2,1)S(1)}, bf16[2,1,1536]{2,1,0:T(2,128)(2,1)S(1)}, u32[]{:S(2)}, u32[]{:S(2)}) collective-permute-start(bf16[2,1,1536]{2,1,0:T(2,128)(2,1)S(1)} %get-tuple-element.9), channel_id=1, source_target_pairs={{1,0},{2,1},{3,2},{4,3},{5,4},{6,5},{7,6},{8,7},{9,8},{10,9},{11,1... | collective-permute-start | bytes 18440 | tf_op jit(solution)/shard_map/ppermute | solution.py:21
Sparse Core Ops, SparseCore 0:
  13.4 60.0 all-gather.4
  75.8 55.8 all-gather.6
  134.0 47.3 all-gather.8
  183.6 52.4 all-gather.10
